TPU v7x, 32 devices: a whole 2x2x4 slice. The times are simulated.
32 devices in a mesh: wide: 4 (over z), grp: 8 (over y, x, core).
Axes of the slice: x: 2, y: 2, z: 4, core: 2. Of those that a mesh axis runs over, the one named last changes fastest.
Arguments:
- amplitudes: bfloat16 [32, 8192], P(('wide', 'grp')), may hold values from -6 to 6
- amplitude_live: int32 [32, 64], replicated, may hold values from 0 to 1, as said below
- integrals: bfloat16 [2048, 8192], P('grp', 'wide'), may hold values from -0.09375 to 0.09375
- integral_live: int32 [16, 64], P('grp', 'wide'), may hold values 0 or 1
Outputs:
- ladder: bfloat16 [32, 2048], P(('wide', 'grp'))
Inputs may be any that keep to these rules, and one draw needn't show every extreme that they name: `amplitude_live`: entries are 0 or 1. In every row b, among the 16 cd tiles c with c // 16 equal to one index of wide, at most 12 are 1; in every row exactly 12 for at least one such index.
All inputs are finite; a program needn't handle non-finite values. No bound on the sum of `integral_live` on one device may be relied on, other than what follows from the above.
Results may differ from a plain program's by a relative error of at most 0.0018.
Values may be sent and summed in bfloat16 or wider, within the bound.
A program may use at most 64 MiB of HBM per device.

v0:
```python
import jax
import jax.numpy as jnp
from jax import lax
from jax.sharding import PartitionSpec as P

TW = 128


def per_device(amplitudes, amplitude_live, integrals, integral_live):
    wide_count = lax.axis_size("wide")
    group_count = lax.axis_size("grp")
    wide_index = lax.axis_index("wide")
    group_index = lax.axis_index("grp")
    row_count = amplitudes.shape[0]
    column_tiles = integrals.shape[1] // TW
    ab_tiles = integrals.shape[0] // TW
    own_live = lax.dynamic_index_in_dim(
        amplitude_live, wide_index * group_count + group_index, 0, keepdims=False
    )
    own_live = own_live.reshape(wide_count, column_tiles)
    amp_view = amplitudes.reshape(row_count, wide_count, column_tiles, TW)
    masked = amp_view * own_live.astype(amplitudes.dtype)[None, :, :, None]
    arrived = lax.all_to_all(
        masked.reshape(row_count, wide_count * column_tiles * TW),
        "wide",
        split_axis=1,
        concat_axis=0,
        tiled=True,
    )
    columns = arrived.reshape(wide_count, row_count, column_tiles * TW)
    int_mask = integral_live.astype(integrals.dtype)
    int_used = (
        integrals.reshape(ab_tiles, TW, column_tiles, TW) * int_mask[:, None, :, None]
    ).reshape(ab_tiles * TW, column_tiles * TW)
    partial_sums = lax.dot_general(
        lax.all_gather(columns, "grp", axis=1, tiled=True),
        int_used,
        (((2,), (1,)), ((), ())),
        preferred_element_type=jnp.float32,
    )
    summed = lax.psum_scatter(partial_sums, "wide", scatter_dimension=0, tiled=True)
    finished = summed.reshape(group_count * row_count, ab_tiles * TW).astype(jnp.bfloat16)
    return lax.all_to_all(finished, "grp", split_axis=0, concat_axis=1, tiled=True)


def solution(mesh):
    in_specs = (P(("wide", "grp"), None), P(), P("grp", "wide"), P("grp", "wide"))
    out_specs = P(("wide", "grp"), None)
    return jax.shard_map(
        per_device, mesh=mesh, in_specs=in_specs, out_specs=out_specs, check_vma=False
    )
```

profile of v0, /device:TPU:0, one launch (start us, length us, event | category | flops | bytes accessed | tf_op | source)
XLA Modules:
  0.0 66.2 jit_solution(11684433662116802342)
XLA Ops:
  6.5 0.0 copy-start.1
  6.5 0.0 copy-start.2
  6.5 0.0 copy-start
  6.5 0.8 %convert_reduce_fusion = bf16[64]{0:T(256)(128)(2,1)S(1)} fusion(s32[32,64]{1,0:T(8,128)} %param.5, s32[]{:T(128)S(6)} %select_n.4), kind=kLoop, calls=%fused_computation.7 | loop fusion | flops 64 | bytes 388 | tf_op jit(solution)/shard_map/convert_element_type | solution.py:22
  7.3 0.1 convert_element_type.27
  7.4 0.1 mul.28
  7.5 0.0 copy-done.1
  7.5 0.1 mul.30
  7.6 0.5 broadcast.11
  8.1 0.7 %reduce.5 = bf16[4,2048]{1,0:T(4,128)(2,1)S(1)} reduce(bf16[4,1,2048]{2,1,0:T(2,128)(2,1)S(1)} %bitcast.22, bf16[]{:T(256)} %broadcast.11), dimensions={1}, to_apply=%bitcast.18.reduce_sub_computation | reduce | bytes 32770
  8.8 0.6 reshape.61
  9.5 6.3 %all-to-all-start = ((bf16[4,2,1024]{2,1,0:T(2,128)(2,1)}), bf16[4,2,1024]{2,1,0:T(2,128)(2,1)S(1)}, u32[]{:S(2)}, u32[]{:S(2)}) async-start(bf16[4,2,1024]{2,1,0:T(2,128)(2,1)} %reshape.61), calls=%async_computation | async-start | bytes 32768 | tf_op jit(solution)/shard_map/all_to_all | solution.py:23
  15.8 0.0 reduce-scatter.2.cloned.1.call-start
  15.8 0.0 copy-done.2
  15.8 5.6 %all-to-all-done = bf16[4,2,1024]{2,1,0:T(2,128)(2,1)S(1)} async-done(((bf16[4,2,1024]{2,1,0:T(2,128)(2,1)}), bf16[4,2,1024]{2,1,0:T(2,128)(2,1)S(1)}, u32[]{:S(2)}, u32[]{:S(2)}) %all-to-all-start) | async-done | bytes 16416 | tf_op jit(solution)/shard_map/all_to_all | solution.py:23
  21.4 9.3 %all-gather = bf16[1,4,16384]{2,0,1:T(2,128)(2,1)S(1)} all-gather(bf16[1,4,2048]{2,0,1:T(2,128)(2,1)S(1)} %bitcast.23), channel_id=2, replica_groups=mesh['wide'=4,'grp'=8] {'grp'}, dimensions={2}, use_global_device_ids=true | all-gather | bytes 147456 | tf_op jit(solution)/shard_map/all_gather | solution.py:36
  30.7 0.8 %reduce.1 = bf16[4,16384]{1,0:T(4,128)(2,1)S(1)} reduce(bf16[1,4,16384]{2,0,1:T(2,128)(2,1)S(1)} %all-gather, bf16[]{:T(256)} %constant.19), dimensions={0}, to_apply=%all-gather.reduce_sub_computation | reduce | bytes 262146 | tf_op jit(solution)/shard_map/all_gather | solution.py:36
  31.5 0.2 mul.31
  31.8 0.0 copy-done
  31.8 1.1 %fusion.1 = f32[4,8,256]{2,1,0:T(8,128)} fusion(bf16[256,2048]{1,0:T(8,128)(2,1)S(1)} %copy-done, bf16[32,8,16,128]{3,2,1,0:T(8,128)(2,1)S(1)} %bitcast.20, bf16[1,4,8,2048]{3,1,2,0:T(4,128)(2,1)S(1)} %bitcast.21), kind=kOutput, calls=%fused_computation.2 | convolution fusion | flops 34078720 | bytes 2260992 | tf_op jit(solution)/shard_map/dot_general | solution.py:35
  32.8 0.0 reduce-scatter.2.cloned.1.call-update
  32.9 16.4 %reduce-scatter.2.cloned.1.call-done = f32[1,8,256]{2,1,0:T(8,128)} async-done(((f32[4,8,256]{2,1,0:T(8,128)}), f32[1,8,256]{2,1,0:T(8,128)}) %reduce-scatter.2.cloned.1.call-update) | async-done | bytes 8208 | tf_op jit(solution)/shard_map/reduce_scatter | solution.py:41
  49.3 0.7 %convert_bitcast_fusion = bf16[8,1,256]{2,0,1:T(8,128)(2,1)S(1)} fusion(f32[1,8,256]{2,1,0:T(8,128)} %reduce-scatter.2.cloned.1.call-done), kind=kLoop, calls=%fused_computation.6 | loop fusion | flops 2048 | bytes 12288 | tf_op jit(solution)/shard_map/convert_element_type | solution.py:42
  50.0 0.6 reduce.6
  50.7 8.1 %all_to_all.26 = bf16[8,2,128]{2,1,0:T(2,128)(2,1)S(1)} all-to-all(bf16[8,2,128]{2,1,0:T(2,128)(2,1)S(1)} %reshape.63), channel_id=1, replica_groups=mesh['wide'=4,'grp'=8] {'grp'}, dimensions={0} | all-to-all | bytes 8192 | tf_op jit(solution)/shard_map/all_to_all | solution.py:43
  58.8 0.6 reshape.64
  (4 shorter events, 0.0 us)
Async XLA Ops:
  6.5 1.0 %copy-start.1 = (bf16[1,8192]{1,0:T(2,128)(2,1)S(1)}, bf16[1,8192]{1,0:T(2,128)(2,1)}, u32[]{:S(2)}) copy-start(bf16[1,8192]{1,0:T(2,128)(2,1)} %param.4) | copy-start | bytes 49156
  6.5 9.2 %copy-start.2 = (s32[2,16]{1,0:T(2,128)S(1)}, s32[2,16]{1,0:T(2,128)}, u32[]{:S(2)}) copy-start(s32[2,16]{1,0:T(2,128)} %param.7) | copy-start | bytes 388
  6.5 25.2 %copy-start = (bf16[256,2048]{1,0:T(8,128)(2,1)S(1)}, bf16[256,2048]{1,0:T(8,128)(2,1)}, u32[]{:S(2)}) copy-start(bf16[256,2048]{1,0:T(8,128)(2,1)} %param.6) | copy-start | bytes 3145732
  9.5 11.9 %all-to-all-start = ((bf16[4,2,1024]{2,1,0:T(2,128)(2,1)}), bf16[4,2,1024]{2,1,0:T(2,128)(2,1)S(1)}, u32[]{:S(2)}, u32[]{:S(2)}) async-start(bf16[4,2,1024]{2,1,0:T(2,128)(2,1)} %reshape.61), calls=%async_computation | async-start | bytes 32768 | tf_op jit(solution)/shard_map/all_to_all | solution.py:23
  15.8 33.5 %reduce-scatter.2.cloned.1.call-start = ((), (), s32[]{:S(2)}) async-start(), calls=%async_computation.3 | async-start | bytes 40960 | tf_op jit(solution)/shard_map/reduce_scatter | solution.py:41
Sparse Core Ops, SparseCore 0:
  33.0 16.2 reduce-scatter.1
where the time goes:
time: 66.6 us; the launch traced here: 66.2 us
  waiting for transfers between devices  22.1 us (33%)
  blocking collectives  17.4 us (26%)
  between operations  13.4 us (20%)
  starting transfers between devices  6.32 us (9%)
  other arithmetic  3.75 us (6%)
  local copies, waits for them, and re-layouts  2.16 us (3%)
  matrix products  1.07 us (2%)
    reduce_scatter x1, waiting for transfers between devices, per_device(): lax.psum_scatter(partial_sums, 'wide', scatter_dimension=0, tiled=True)  16.4 us
    all_gather x1, blocking collectives, per_device(): lax.all_gather(columns, 'grp', axis=1, tiled=True)  9.32 us
    all_to_all x1, blocking collectives, per_device(): lax.all_to_all(finished, 'grp', split_axis=0, concat_axis=1, tiled=True)  8.12 us
    all_to_all x1, starting transfers between devices, per_device(): lax.all_to_all(masked.reshape(row_count, wide_count * column_tiles * TW),...  6.32 us
    all_to_all x1, waiting for transfers between devices, per_device(): lax.all_to_all(masked.reshape(row_count, wide_count * column_tiles * TW),...  5.6 us
    unnamed x11, local copies, waits for them, and re-layouts  1.77 us
    convert_element_type x2, other arithmetic, per_device(): summed.reshape(group_count * row_count, ab_tiles * TW).astype(jnp.bfloat16)  1.35 us
  transfers between devices with their start and end apart: 2, of which 2 were waited for; matrix products, arithmetic and copies ran while one was open for 0% of the time, Pallas kernels for 0%

commit v1 on v0

v1 whole, which is shorter than its diff:
```python
import functools

import jax
import jax.numpy as jnp
from jax import lax
from jax.experimental import pallas as pl
from jax.experimental.pallas import tpu as pltpu
from jax.sharding import PartitionSpec as P

TW = 128
MESH = pl.DeviceIdType.MESH


def loop(count, body, limit=32):
    if count <= limit:
        for i in range(count):
            body(i)
    else:
        lax.fori_loop(0, count, lambda i, c: (body(i), c)[1], 0)


def kernel(
    n_wide, n_grp,
    amp_hbm, live_hbm, int_hbm, int_live_hbm, out_ref,
    amp, live, ints, int_live, tiles, send_buf, recv_buf, wide_tiles, lhs,
    partial, rows_in,
    load_sems, send_sem, recv_sem, send2_sem, recv2_sem,
):
    n = n_wide * n_grp
    cd_tiles = ints.shape[1] // TW
    ab_tiles = ints.shape[0] // TW
    ab = ints.shape[0]
    wide = lax.axis_index("wide")
    grp = lax.axis_index("grp")
    me = wide * n_grp + grp

    slab = pl.multiple_of((me // 8) * 8, 8)
    loads = [
        pltpu.make_async_copy(amp_hbm, amp, load_sems.at[0]),
        pltpu.make_async_copy(live_hbm.at[pl.ds(slab, 8), :], live, load_sems.at[1]),
        pltpu.make_async_copy(int_live_hbm, int_live, load_sems.at[2]),
        pltpu.make_async_copy(int_hbm, ints, load_sems.at[3]),
    ]
    for load in loads:
        load.start()

    barrier = pltpu.get_barrier_semaphore()

    def place(i):
        other = lax.rem(me + i, n)
        return other, (other // n_grp, lax.rem(other, n_grp))

    def greet(i):
        _, where = place(i + 1)
        pl.semaphore_signal(barrier, inc=1, device_id=where, device_id_type=MESH)

    loop(n - 1, greet)

    loads[0].wait()
    loads[1].wait()
    my_row = lax.rem(me, 8)

    def prepare(w):
        for c in range(cd_tiles):
            t = w * cd_tiles + c
            column = t * TW if isinstance(w, int) else pl.multiple_of(t * TW, TW)
            row = amp[:, pl.ds(column, TW)].astype(jnp.float32)
            tiles[c:c + 1, :] = row * live[my_row, t].astype(jnp.float32)
        send_buf[w] = tiles[...].astype(jnp.bfloat16)

    loop(n_wide, prepare, 4)

    pl.semaphore_wait(barrier, n - 1)

    def send(i):
        other, where = place(i + 1)
        pltpu.make_async_remote_copy(
            src_ref=send_buf.at[other // n_grp],
            dst_ref=recv_buf.at[me],
            send_sem=send_sem,
            recv_sem=recv_sem,
            device_id=where,
            device_id_type=MESH,
        ).start()

    loop(n - 1, send)
    recv_buf[me] = send_buf[wide]

    loads[2].wait()
    loads[3].wait()
    for a in range(ab_tiles):
        for c in range(cd_tiles):
            block = (slice(a * TW, (a + 1) * TW), slice(c * TW, (c + 1) * TW))
            keep = jnp.full((TW, TW), int_live[a, c].astype(jnp.float32), jnp.float32)
            ints[block] = ints[block] * keep.astype(jnp.bfloat16)

    others = recv_buf.at[pl.ds(0, n - 1)]
    pltpu.make_async_copy(others, others, recv_sem).wait()

    step = min(n, 32)

    def multiply(r):
        first = r * step
        wide_tiles[...] = (
            recv_buf[pl.ds(first, step)].astype(jnp.float32).reshape(step * cd_tiles, TW)
        )
        for c in range(cd_tiles):
            lhs[:, c * TW:(c + 1) * TW] = wide_tiles[
                pl.ds(c, step, stride=cd_tiles), :
            ].astype(jnp.bfloat16)
        total = lax.dot_general(
            lhs[...], ints[...], (((1,), (1,)), ((), ())),
            preferred_element_type=jnp.float32,
        )
        partial[pl.ds(first, step)] = total.reshape(step, 1, ab)

    loop(n // step, multiply, 1)

    def send_row(i):
        other, where = place(i + 1)
        pltpu.make_async_remote_copy(
            src_ref=partial.at[other],
            dst_ref=rows_in.at[me],
            send_sem=send2_sem,
            recv_sem=recv2_sem,
            device_id=where,
            device_id_type=MESH,
        ).start()

    loop(n - 1, send_row)
    rows_in[me] = partial[me]
    other_rows = rows_in.at[pl.ds(0, n - 1)]
    pltpu.make_async_copy(other_rows, other_rows, recv2_sem).wait()

    for g in range(n_grp):
        if n_wide <= 8:
            total = rows_in[g]
            for w in range(1, n_wide):
                total = total + rows_in[w * n_grp + g]
        else:
            total = lax.fori_loop(
                1, n_wide, lambda w, s: s + rows_in[w * n_grp + g], rows_in[g]
            )
        out_ref[:, g * ab:(g + 1) * ab] = total.astype(jnp.bfloat16)

    pltpu.make_async_copy(others, others, send_sem).wait()
    pltpu.make_async_copy(other_rows, other_rows, send2_sem).wait()


def per_device(amplitudes, amplitude_live, integrals, integral_live):
    n_wide = lax.axis_size("wide")
    n_grp = lax.axis_size("grp")
    n = n_wide * n_grp
    ab, cd = integrals.shape
    cd_tiles = cd // TW
    step = min(n, 32)
    bf16, f32 = jnp.bfloat16, jnp.float32
    anywhere = pl.BlockSpec(memory_space=pl.ANY)
    return pl.pallas_call(
        functools.partial(kernel, n_wide, n_grp),
        out_shape=jax.ShapeDtypeStruct((1, n_grp * ab), bf16),
        in_specs=[anywhere] * 4,
        out_specs=pl.BlockSpec(memory_space=pltpu.VMEM),
        scratch_shapes=[
            pltpu.VMEM(amplitudes.shape, bf16),
            pltpu.SMEM((8, amplitude_live.shape[1]), jnp.int32),
            pltpu.VMEM((ab, cd), bf16),
            pltpu.SMEM(integral_live.shape, jnp.int32),
            pltpu.VMEM((cd_tiles, TW), f32),
            pltpu.VMEM((n_wide, cd_tiles, TW), bf16),
            pltpu.VMEM((n, cd_tiles, TW), bf16),
            pltpu.VMEM((step * cd_tiles, TW), f32),
            pltpu.VMEM((step, cd), bf16),
            pltpu.VMEM((n, 1, ab), f32),
            pltpu.VMEM((n, 1, ab), f32),
            pltpu.SemaphoreType.DMA((4,)),
            pltpu.SemaphoreType.DMA,
            pltpu.SemaphoreType.DMA,
            pltpu.SemaphoreType.DMA,
            pltpu.SemaphoreType.DMA,
        ],
        compiler_params=pltpu.CompilerParams(
            collective_id=0, has_side_effects=True, vmem_limit_bytes=48 * 1024 * 1024
        ),
        cost_estimate=pl.CostEstimate(
            flops=2 * n * ab * cd, bytes_accessed=2 * ab * cd, transcendentals=0
        ),
    )(amplitudes, amplitude_live, integrals, integral_live)


def solution(mesh):
    in_specs = (P(("wide", "grp"), None), P(), P("grp", "wide"), P("grp", "wide"))
    out_specs = P(("wide", "grp"), None)
    return jax.shard_map(
        per_device, mesh=mesh, in_specs=in_specs, out_specs=out_specs, check_vma=False
    )
```

time: 66.6 us -> 22.1 us (0.33)
  waiting for transfers between devices: 22.1 us -> 0 us
  Pallas kernels: 0 us -> 17.8 us
  blocking collectives: 17.4 us -> 0 us
  between operations: 13.4 us -> 0.01 us
  starting transfers between devices: 6.32 us -> 0 us
  other arithmetic: 3.75 us -> 0 us
  local copies, waits for them, and re-layouts: 2.16 us -> 3.98 us
  matrix products: 1.07 us -> 0 us
    pallas_call x0 -> x1, Pallas kernels: none -> 17.8 us  [per_device(): pl.pallas_call(functools.partial(kernel, n_wide, n_grp), out_shape=jax.Sh...]
    reduce_scatter x1 -> x0, waiting for transfers between devices: 16.4 us -> none  [per_device(): lax.psum_scatter(partial_sums, 'wide', scatter_dimension=0, tiled=True)]
    all_gather x1 -> x0, blocking collectives: 9.32 us -> none  [per_device(): lax.all_gather(columns, 'grp', axis=1, tiled=True)]
    all_to_all x1 -> x0, blocking collectives: 8.12 us -> none  [per_device(): lax.all_to_all(finished, 'grp', split_axis=0, concat_axis=1, tiled=True)]
    all_to_all x1 -> x0, starting transfers between devices: 6.32 us -> none  [per_device(): lax.all_to_all(masked.reshape(row_count, wide_count * column_tiles * TW),...]
    all_to_all x1 -> x0, waiting for transfers between devices: 5.6 us -> none  [per_device(): lax.all_to_all(masked.reshape(row_count, wide_count * column_tiles * TW),...]
    unnamed x11 -> x9, local copies, waits for them, and re-layouts: 1.77 us -> 3.98 us
    convert_element_type x4 -> x0, other arithmetic: 2.15 us -> none  [the longest x2 1.35 us: per_device(): summed.reshape(group_count * row_count, ab_tiles * TW).astype(jnp.bfloat16)]
  transfers between devices with their start and end apart: 2 -> 0, of which waited for: 2 -> 0; matrix products, arithmetic and copies ran while one was open for 0% -> 0% of each run, Pallas kernels for 0% -> 0%
where the time goes in v1:
time: 22.1 us; the launch traced here: 21.8 us
  Pallas kernels  17.8 us (81%)
  local copies, waits for them, and re-layouts  3.98 us (18%)
    pallas_call x1, Pallas kernels, per_device(): pl.pallas_call(functools.partial(kernel, n_wide, n_grp), out_shape=jax.Sh...  17.8 us
    unnamed x9, local copies, waits for them, and re-layouts  3.98 us

profile of v1, /device:TPU:0, one launch (start us, length us, event | category | flops | bytes accessed | tf_op | source)
XLA Modules:
  0.0 21.8 jit_solution(3277924960270271460)
XLA Ops:
  0.0 0.0 copy-start
  0.0 1.2 %copy-done = bf16[256,2048]{1,0:T(8,128)(2,1)S(1)} copy-done((bf16[256,2048]{1,0:T(8,128)(2,1)S(1)}, bf16[256,2048]{1,0:T(8,128)(2,1)}, u32[]{:S(2)}) %copy-start) | copy-done | bytes 1048600
  1.2 0.0 copy-start.1
  1.2 0.8 %copy-done.1 = bf16[1,8192]{1,0:T(2,128)(2,1)S(1)} copy-done((bf16[1,8192]{1,0:T(2,128)(2,1)S(1)}, bf16[1,8192]{1,0:T(2,128)(2,1)}, u32[]{:S(2)}) %copy-start.1) | copy-done | bytes 16408
  2.0 0.0 copy-start.2
  2.0 0.7 %copy-done.2 = s32[32,64]{1,0:T(8,128)S(1)} copy-done((s32[32,64]{1,0:T(8,128)S(1)}, s32[32,64]{1,0:T(8,128)}, u32[]{:S(2)}) %copy-start.2) | copy-done | bytes 8216
  2.7 0.0 copy-start.3
  2.7 0.7 %copy-done.3 = s32[2,16]{1,0:T(2,128)S(1)} copy-done((s32[2,16]{1,0:T(2,128)S(1)}, s32[2,16]{1,0:T(2,128)}, u32[]{:S(2)}) %copy-start.3) | copy-done | bytes 152
  3.4 17.8 %shard_map.46 = bf16[1,2048]{1,0:T(2,128)(2,1)S(1)} custom-call(bf16[1,8192]{1,0:T(2,128)(2,1)S(1)} %copy-done.1, s32[32,64]{1,0:T(8,128)S(1)} %copy-done.2, bf16[256,2048]{1,0:T(8,128)(2,1)S(1)} %copy-done, s32[2,16]{1,0:T(2,128)S(1)} %copy-done.3), custom_call_target="tpu_custom_call" | custom-call | flops 33554432 | bytes 1048576 | tf_op jit(solution)/shard_map/pallas_call | solution.py:159
  21.2 0.6 %copy.6 = bf16[1,2048]{1,0:T(2,128)(2,1)} copy(bf16[1,2048]{1,0:T(2,128)(2,1)S(1)} %shard_map.46) | data formatting | bytes 8192
Async XLA Ops:
  0.0 1.2 %copy-start = (bf16[256,2048]{1,0:T(8,128)(2,1)S(1)}, bf16[256,2048]{1,0:T(8,128)(2,1)}, u32[]{:S(2)}) copy-start(bf16[256,2048]{1,0:T(8,128)(2,1)} %int_hbm.1) | copy-start | bytes 3145732
  1.2 0.8 %copy-start.1 = (bf16[1,8192]{1,0:T(2,128)(2,1)S(1)}, bf16[1,8192]{1,0:T(2,128)(2,1)}, u32[]{:S(2)}) copy-start(bf16[1,8192]{1,0:T(2,128)(2,1)} %amp_hbm.1) | copy-start | bytes 49156
  2.0 0.7 %copy-start.2 = (s32[32,64]{1,0:T(8,128)S(1)}, s32[32,64]{1,0:T(8,128)}, u32[]{:S(2)}) copy-start(s32[32,64]{1,0:T(8,128)} %live_hbm.1) | copy-start | bytes 24580
  2.7 0.7 %copy-start.3 = (s32[2,16]{1,0:T(2,128)S(1)}, s32[2,16]{1,0:T(2,128)}, u32[]{:S(2)}) copy-start(s32[2,16]{1,0:T(2,128)} %int_live_hbm.1) | copy-start | bytes 388

commit v2 on v1

v2 whole, which is shorter than its diff:
```python
import functools

import jax
import jax.numpy as jnp
from jax import lax
from jax.experimental import pallas as pl
from jax.experimental.pallas import tpu as pltpu
from jax.sharding import PartitionSpec as P

TW = 128
MESH = pl.DeviceIdType.MESH


def loop(count, body, limit):
    if count <= limit:
        for i in range(count):
            body(i)
    else:
        lax.fori_loop(0, count, lambda i, c: (body(i), c)[1], 0)


def kernel(
    n_wide, n_grp,
    amp_hbm, live_hbm, int_hbm, int_live_hbm, out_ref,
    amp, live, ints, int_live, tiles, send_buf, blocks, wide_tiles, lhs,
    partial, slabs, rows,
    load_sems, send_sems, recv_sems,
):
    ab, cd = ints.shape
    cd_tiles, ab_tiles = cd // TW, ab // TW
    wide = lax.axis_index("wide")
    grp = lax.axis_index("grp")
    my_row = lax.rem(wide * n_grp + grp, 8)

    slab = pl.multiple_of(((wide * n_grp + grp) // 8) * 8, 8)
    loads = [
        pltpu.make_async_copy(amp_hbm, amp, load_sems.at[0]),
        pltpu.make_async_copy(live_hbm.at[pl.ds(slab, 8), :], live, load_sems.at[1]),
        pltpu.make_async_copy(int_live_hbm, int_live, load_sems.at[2]),
        pltpu.make_async_copy(int_hbm, ints, load_sems.at[3]),
    ]
    for load in loads:
        load.start()

    barrier = pltpu.get_barrier_semaphore()

    def after(index, i, count):
        there = index + i
        return jnp.where(there >= count, there - count, there)

    def over_wide(body):
        def one(i):
            there = after(wide, i + 1, n_wide)
            body(there, (there, grp))
        loop(n_wide - 1, one, 8)

    def over_grp(body):
        for i in range(1, n_grp):
            there = after(grp, i, n_grp)
            body(there, (wide, there))

    def greet(_, where):
        pl.semaphore_signal(barrier, inc=1, device_id=where, device_id_type=MESH)

    over_wide(greet)
    over_grp(greet)

    loads[0].wait()
    loads[1].wait()

    def prepare(w):
        for c in range(cd_tiles):
            t = w * cd_tiles + c
            column = t * TW if isinstance(w, int) else pl.multiple_of(t * TW, TW)
            row = amp[:, pl.ds(column, TW)].astype(jnp.float32)
            tiles[c:c + 1, :] = row * live[my_row, t].astype(jnp.float32)
        send_buf[w] = tiles[...].astype(jnp.bfloat16)

    loop(n_wide, prepare, 4)

    pl.semaphore_wait(barrier, n_wide + n_grp - 2)

    def send(stage, src, dst, where):
        pltpu.make_async_remote_copy(
            src_ref=src,
            dst_ref=dst,
            send_sem=send_sems.at[stage],
            recv_sem=recv_sems.at[stage],
            device_id=where,
            device_id_type=MESH,
        ).start()

    def wait_all(refs, sem):
        pltpu.make_async_copy(refs, refs, sem).wait()

    over_wide(lambda w, where: send(0, send_buf.at[w], blocks.at[grp, wide], where))
    blocks[grp, wide] = send_buf[wide]

    loads[2].wait()
    loads[3].wait()
    for a in range(ab_tiles):
        for c in range(cd_tiles):
            block = (slice(a * TW, (a + 1) * TW), slice(c * TW, (c + 1) * TW))
            keep = jnp.full((TW, TW), int_live[a, c].astype(jnp.float32), jnp.float32)
            ints[block] = ints[block] * keep.astype(jnp.bfloat16)

    from_wide = blocks.at[0, pl.ds(0, n_wide - 1)]
    wait_all(from_wide, recv_sems.at[0])
    over_grp(lambda _, where: send(1, blocks.at[grp], blocks.at[grp], where))
    from_grp = blocks.at[pl.ds(0, n_grp - 1)]
    wait_all(from_grp, recv_sems.at[1])

    step = min(n_wide, 4)

    def multiply(r):
        first = r * step
        for g in range(n_grp):
            wide_tiles[g] = (
                blocks[g, pl.ds(first, step)].astype(jnp.float32).reshape(step * cd_tiles, TW)
            )
        flat = wide_tiles.reshape(n_grp * step * cd_tiles, TW)
        for w in range(step):
            for c in range(0, cd_tiles):
                lhs[w * n_grp:(w + 1) * n_grp, c * TW:(c + 1) * TW] = flat[
                    pl.ds(w * cd_tiles + c, n_grp, stride=step * cd_tiles), :
                ]
        total = lax.dot_general(
            lhs[...].astype(jnp.bfloat16), ints[...], (((1,), (1,)), ((), ())),
            preferred_element_type=jnp.float32,
        )
        partial[pl.ds(first, step)] = total.reshape(step, n_grp, ab)

    loop(n_wide // step, multiply, 1)

    over_wide(lambda w, where: send(2, partial.at[w], slabs.at[wide], where))
    slabs[wide] = partial[wide]
    from_wide_slabs = slabs.at[pl.ds(0, n_wide - 1)]
    wait_all(from_wide_slabs, recv_sems.at[2])
    if n_wide <= 8:
        total = slabs[0]
        for w in range(1, n_wide):
            total = total + slabs[w]
    else:
        total = lax.fori_loop(1, n_wide, lambda w, s: s + slabs[w], slabs[0])
    for g in range(n_grp):
        rows[g] = total[g:g + 1, :]
    columns = pl.ds(pl.multiple_of(grp * ab, ab), ab)
    own = pltpu.make_async_copy(rows.at[grp], out_ref.at[:, columns], load_sems.at[0])
    own.start()
    over_grp(lambda g, where: send(3, rows.at[g], out_ref.at[:, columns], where))
    from_grp_rows = out_ref.at[:, pl.ds(0, (n_grp - 1) * ab)]
    wait_all(from_grp_rows, recv_sems.at[3])
    own.wait()

    wait_all(from_wide, send_sems.at[0])
    wait_all(from_grp, send_sems.at[1])
    wait_all(from_wide_slabs, send_sems.at[2])
    wait_all(rows.at[pl.ds(0, n_grp - 1)], send_sems.at[3])


def per_device(amplitudes, amplitude_live, integrals, integral_live):
    n_wide = lax.axis_size("wide")
    n_grp = lax.axis_size("grp")
    ab, cd = integrals.shape
    cd_tiles = cd // TW
    step = min(n_wide, 4)
    bf16, f32 = jnp.bfloat16, jnp.float32
    anywhere = pl.BlockSpec(memory_space=pl.ANY)
    finished = pl.pallas_call(
        functools.partial(kernel, n_wide, n_grp),
        out_shape=jax.ShapeDtypeStruct((1, n_grp * ab), f32),
        in_specs=[anywhere] * 4,
        out_specs=anywhere,
        scratch_shapes=[
            pltpu.VMEM(amplitudes.shape, bf16),
            pltpu.SMEM((8, amplitude_live.shape[1]), jnp.int32),
            pltpu.VMEM((ab, cd), bf16),
            pltpu.SMEM(integral_live.shape, jnp.int32),
            pltpu.VMEM((cd_tiles, TW), f32),
            pltpu.VMEM((n_wide, cd_tiles, TW), bf16),
            pltpu.VMEM((n_grp, n_wide, cd_tiles, TW), bf16),
            pltpu.VMEM((n_grp, step * cd_tiles, TW), f32),
            pltpu.VMEM((n_grp * step, cd), f32),
            pltpu.VMEM((n_wide, n_grp, ab), f32),
            pltpu.VMEM((n_wide, n_grp, ab), f32),
            pltpu.VMEM((n_grp, 1, ab), f32),
            pltpu.SemaphoreType.DMA((4,)),
            pltpu.SemaphoreType.DMA((4,)),
            pltpu.SemaphoreType.DMA((4,)),
        ],
        compiler_params=pltpu.CompilerParams(
            collective_id=0, has_side_effects=True, vmem_limit_bytes=60 * 1024 * 1024
        ),
        cost_estimate=pl.CostEstimate(
            flops=2 * n_wide * n_grp * ab * cd, bytes_accessed=2 * ab * cd, transcendentals=0
        ),
    )(amplitudes, amplitude_live, integrals, integral_live)
    return finished.astype(bf16)


def solution(mesh):
    in_specs = (P(("wide", "grp"), None), P(), P("grp", "wide"), P("grp", "wide"))
    out_specs = P(("wide", "grp"), None)
    return jax.shard_map(
        per_device, mesh=mesh, in_specs=in_specs, out_specs=out_specs, check_vma=False
    )
```

time: 22.1 us -> 21 us (0.950)
  local copies, waits for them, and re-layouts: 3.98 us -> 0 us
  Pallas kernels: 17.8 us -> 19.5 us
  other arithmetic: 0 us -> 1.3 us
    unnamed x9 -> x0, local copies, waits for them, and re-layouts: 3.98 us -> none
    pallas_call x1, Pallas kernels: 17.8 us -> 19.5 us  [per_device(): pl.pallas_call(functools.partial(kernel, n_wide, n_grp), out_shape=jax.Sh...]
    convert_element_type x0 -> x1, other arithmetic: none -> 1.3 us  [per_device(): return finished.astype(bf16)]
where the time goes in v2:
time: 21 us; the launch traced here: 20.8 us
  Pallas kernels  19.5 us (93%)
  other arithmetic  1.3 us (6%)
    pallas_call x1, Pallas kernels, per_device(): pl.pallas_call(functools.partial(kernel, n_wide, n_grp), out_shape=jax.Sh...  19.5 us
    convert_element_type x1, other arithmetic, per_device(): return finished.astype(bf16)  1.3 us

profile of v2, /device:TPU:0, one launch (start us, length us, event | category | flops | bytes accessed | tf_op | source)
XLA Modules:
  0.0 20.8 jit_solution(17391702371028417016)
XLA Ops:
  0.0 19.5 %shard_map.46 = f32[1,2048]{1,0:T(1,128)} custom-call(bf16[1,8192]{1,0:T(2,128)(2,1)} %amp_hbm.1, s32[32,64]{1,0:T(8,128)} %live_hbm.1, bf16[256,2048]{1,0:T(8,128)(2,1)} %int_hbm.1, s32[2,16]{1,0:T(2,128)} %int_live_hbm.1), custom_call_target="tpu_custom_call" | custom-call | flops 33554432 | bytes 1048576 | tf_op jit(solution)/shard_map/pallas_call | solution.py:169
  19.5 1.3 %convert_element_type.3 = bf16[1,2048]{1,0:T(2,128)(2,1)} convert(f32[1,2048]{1,0:T(1,128)} %shard_map.46) | non-fusion elementwise | flops 2048 | bytes 12288 | tf_op jit(solution)/shard_map/convert_element_type | solution.py:198

commit v3 on v1

v3 whole, which is shorter than its diff:
```python
import functools

import jax
import jax.numpy as jnp
from jax import lax
from jax.experimental import pallas as pl
from jax.experimental.pallas import tpu as pltpu
from jax.sharding import PartitionSpec as P

TW = 128
MESH = pl.DeviceIdType.MESH


def loop(count, body, limit):
    if count <= limit:
        for i in range(count):
            body(i)
    else:
        lax.fori_loop(0, count, lambda i, c: (body(i), c)[1], 0)


def kernel(
    n_wide, n_grp,
    amp_hbm, live_hbm, int_hbm, int_live_hbm, out_ref,
    amp, live, ints, int_live, tiles, send_buf, blocks, wide_tiles, lhs,
    partial, rows_in,
    load_sems, recv_sems, row_sem, send_sems,
):
    ab, cd = ints.shape
    cd_tiles, ab_tiles = cd // TW, ab // TW
    wide = lax.axis_index("wide")
    grp = lax.axis_index("grp")
    my_row = lax.rem(wide * n_grp + grp, 8)

    slab = pl.multiple_of(((wide * n_grp + grp) // 8) * 8, 8)
    loads = [
        pltpu.make_async_copy(amp_hbm, amp, load_sems.at[0]),
        pltpu.make_async_copy(live_hbm.at[pl.ds(slab, 8), :], live, load_sems.at[1]),
        pltpu.make_async_copy(int_live_hbm, int_live, load_sems.at[2]),
        pltpu.make_async_copy(int_hbm, ints, load_sems.at[3]),
    ]
    for load in loads:
        load.start()

    barrier = pltpu.get_barrier_semaphore()

    def up(index, i, count):
        there = index + i
        return jnp.where(there >= count, there - count, there)

    def down(index, i, count):
        there = index - i
        return jnp.where(there < 0, there + count, there)

    near = [up(grp, i, n_grp) for i in range(n_grp)]

    def plane(w, body, first):
        for g in near[first:]:
            body(w, g)

    def greet(w, g):
        pl.semaphore_signal(barrier, inc=1, device_id=(w, g), device_id_type=MESH)

    loop(n_wide - 1, lambda i: plane(up(wide, i + 1, n_wide), greet, 0), 8)
    plane(wide, greet, 1)

    loads[0].wait()
    loads[1].wait()

    def prepare(w):
        for c in range(cd_tiles):
            t = w * cd_tiles + c
            column = t * TW if isinstance(w, int) else pl.multiple_of(t * TW, TW)
            row = amp[:, pl.ds(column, TW)].astype(jnp.float32)
            tiles[c:c + 1, :] = row * live[my_row, t].astype(jnp.float32)
        send_buf[w] = tiles[...].astype(jnp.bfloat16)

    loop(n_wide, prepare, 4)

    pl.semaphore_wait(barrier, n_wide * n_grp - 1)

    def send(w, g):
        pltpu.make_async_remote_copy(
            src_ref=send_buf.at[w],
            dst_ref=blocks.at[wide, grp],
            send_sem=send_sems.at[0],
            recv_sem=recv_sems.at[wide],
            device_id=(w, g),
            device_id_type=MESH,
        ).start()

    def send_row(w, g):
        pltpu.make_async_remote_copy(
            src_ref=partial.at[w, g],
            dst_ref=rows_in.at[wide, grp],
            send_sem=send_sems.at[1],
            recv_sem=row_sem,
            device_id=(w, g),
            device_id_type=MESH,
        ).start()

    def wait_all(refs, sem):
        pltpu.make_async_copy(refs, refs, sem).wait()

    loop(n_wide - 1, lambda i: plane(down(wide, i + 1, n_wide), send, 0), 8)
    plane(wide, send, 1)
    blocks[wide, grp] = send_buf[wide]

    loads[2].wait()
    loads[3].wait()
    for a in range(ab_tiles):
        for c in range(cd_tiles):
            block = (slice(a * TW, (a + 1) * TW), slice(c * TW, (c + 1) * TW))
            keep = jnp.full((TW, TW), int_live[a, c].astype(jnp.float32), jnp.float32)
            ints[block] = ints[block] * keep.astype(jnp.bfloat16)

    def multiply(w):
        wide_tiles[...] = blocks[w].astype(jnp.float32).reshape(n_grp * cd_tiles, TW)
        for c in range(cd_tiles):
            lhs[:, c * TW:(c + 1) * TW] = wide_tiles[
                pl.ds(c, n_grp, stride=cd_tiles), :
            ]
        total = lax.dot_general(
            lhs[...].astype(jnp.bfloat16), ints[...], (((1,), (1,)), ((), ())),
            preferred_element_type=jnp.float32,
        )
        partial[w] = total.reshape(n_grp, 1, ab)

    wait_all(blocks.at[0, pl.ds(0, n_grp - 1)], recv_sems.at[wide])
    multiply(wide)
    plane(wide, send_row, 1)
    rows_in[wide, grp] = partial[wide, grp]

    def other_rows(i):
        w = down(wide, i + 1, n_wide)
        wait_all(blocks.at[0], recv_sems.at[w])
        multiply(w)
        plane(w, send_row, 0)

    loop(n_wide - 1, other_rows, 8)

    def wait_others(refs, sem):
        flat = refs.reshape((n_wide * n_grp,) + refs.shape[2:])
        wait_all(flat.at[pl.ds(0, n_wide * n_grp - 1)], sem)

    wait_others(rows_in, row_sem)
    for g in range(n_grp):
        if n_wide <= 8:
            total = rows_in[0, g]
            for w in range(1, n_wide):
                total = total + rows_in[w, g]
        else:
            total = lax.fori_loop(
                1, n_wide, lambda w, s: s + rows_in[w, g], rows_in[0, g]
            )
        out_ref[:, g * ab:(g + 1) * ab] = total.astype(jnp.bfloat16)

    wait_others(blocks, send_sems.at[0])
    wait_others(rows_in, send_sems.at[1])


def per_device(*args):
    amplitudes, amplitude_live, integrals, integral_live = [
        pltpu.with_memory_space_constraint(x, pltpu.HBM) for x in args
    ]
    n_wide = lax.axis_size("wide")
    n_grp = lax.axis_size("grp")
    ab, cd = integrals.shape
    cd_tiles = cd // TW
    bf16, f32 = jnp.bfloat16, jnp.float32
    return pl.pallas_call(
        functools.partial(kernel, n_wide, n_grp),
        out_shape=jax.ShapeDtypeStruct((1, n_grp * ab), bf16),
        in_specs=[pl.BlockSpec(memory_space=pl.ANY)] * 4,
        out_specs=pl.BlockSpec(memory_space=pltpu.VMEM),
        scratch_shapes=[
            pltpu.VMEM(amplitudes.shape, bf16),
            pltpu.SMEM((8, amplitude_live.shape[1]), jnp.int32),
            pltpu.VMEM((ab, cd), bf16),
            pltpu.SMEM(integral_live.shape, jnp.int32),
            pltpu.VMEM((cd_tiles, TW), f32),
            pltpu.VMEM((n_wide, cd_tiles, TW), bf16),
            pltpu.VMEM((n_wide, n_grp, cd_tiles, TW), bf16),
            pltpu.VMEM((n_grp * cd_tiles, TW), f32),
            pltpu.VMEM((n_grp, cd), f32),
            pltpu.VMEM((n_wide, n_grp, 1, ab), f32),
            pltpu.VMEM((n_wide, n_grp, 1, ab), f32),
            pltpu.SemaphoreType.DMA((4,)),
            pltpu.SemaphoreType.DMA((n_wide,)),
            pltpu.SemaphoreType.DMA,
            pltpu.SemaphoreType.DMA((2,)),
        ],
        compiler_params=pltpu.CompilerParams(
            collective_id=0, has_side_effects=True, vmem_limit_bytes=48 * 1024 * 1024
        ),
        cost_estimate=pl.CostEstimate(
            flops=2 * n_wide * n_grp * ab * cd, bytes_accessed=2 * ab * cd, transcendentals=0
        ),
    )(amplitudes, amplitude_live, integrals, integral_live)


def solution(mesh):
    in_specs = (P(("wide", "grp"), None), P(), P("grp", "wide"), P("grp", "wide"))
    out_specs = P(("wide", "grp"), None)
    return jax.shard_map(
        per_device, mesh=mesh, in_specs=in_specs, out_specs=out_specs, check_vma=False
    )
```

time: 22.1 us -> 18.5 us (0.84)
  local copies, waits for them, and re-layouts: 3.98 us -> 0.6 us
    unnamed x9 -> x1, local copies, waits for them, and re-layouts: 3.98 us -> 0.6 us
where the time goes in v3:
time: 18.5 us; the launch traced here: 18.4 us
  Pallas kernels  17.8 us (96%)
  local copies, waits for them, and re-layouts  0.6 us (3%)
    pallas_call x1, Pallas kernels, per_device(): pl.pallas_call(functools.partial(kernel, n_wide, n_grp), out_shape=jax.Sh...  17.8 us
    unnamed x1, local copies, waits for them, and re-layouts  0.6 us

profile of v3, /device:TPU:0, one launch (start us, length us, event | category | flops | bytes accessed | tf_op | source)
XLA Modules:
  0.0 18.4 jit_solution(17450113025488134305)
XLA Ops:
  0.0 17.8 %shard_map.46 = bf16[1,2048]{1,0:T(2,128)(2,1)S(1)} custom-call(bf16[1,8192]{1,0:T(2,128)(2,1)} %amp_hbm.1, s32[32,64]{1,0:T(8,128)} %live_hbm.1, bf16[256,2048]{1,0:T(8,128)(2,1)} %int_hbm.1, s32[2,16]{1,0:T(2,128)} %int_live_hbm.1), custom_call_target="tpu_custom_call" | custom-call | flops 33554432 | bytes 1048576 | tf_op jit(solution)/shard_map/pallas_call | solution.py:171
  17.8 0.6 %copy.6 = bf16[1,2048]{1,0:T(2,128)(2,1)} copy(bf16[1,2048]{1,0:T(2,128)(2,1)S(1)} %shard_map.46) | data formatting | bytes 8192

commit v4 on v3

--- a/solution.py
+++ b/solution.py
@@ -22,7 +22,7 @@
 def kernel(
     n_wide, n_grp,
     amp_hbm, live_hbm, int_hbm, int_live_hbm, out_ref,
-    amp, live, ints, int_live, tiles, send_buf, blocks, wide_tiles, lhs,
+    amp, live, ints, ints_t, int_live, tiles, send_buf, blocks, wide_tiles, lhs,
     partial, rows_in,
     load_sems, recv_sems, row_sem, send_sems,
 ):
@@ -112,7 +112,7 @@
         for c in range(cd_tiles):
             block = (slice(a * TW, (a + 1) * TW), slice(c * TW, (c + 1) * TW))
             keep = jnp.full((TW, TW), int_live[a, c].astype(jnp.float32), jnp.float32)
-            ints[block] = ints[block] * keep.astype(jnp.bfloat16)
+            ints_t[block[1], block[0]] = (ints[block] * keep.astype(jnp.bfloat16)).T
 
     def multiply(w):
         wide_tiles[...] = blocks[w].astype(jnp.float32).reshape(n_grp * cd_tiles, TW)
@@ -121,7 +121,7 @@
                 pl.ds(c, n_grp, stride=cd_tiles), :
             ]
         total = lax.dot_general(
-            lhs[...].astype(jnp.bfloat16), ints[...], (((1,), (1,)), ((), ())),
+            lhs[...].astype(jnp.bfloat16), ints_t[...], (((1,), (0,)), ((), ())),
             preferred_element_type=jnp.float32,
         )
         partial[w] = total.reshape(n_grp, 1, ab)
@@ -177,6 +177,7 @@
             pltpu.VMEM(amplitudes.shape, bf16),
             pltpu.SMEM((8, amplitude_live.shape[1]), jnp.int32),
             pltpu.VMEM((ab, cd), bf16),
+            pltpu.VMEM((cd, ab), bf16),
             pltpu.SMEM(integral_live.shape, jnp.int32),
             pltpu.VMEM((cd_tiles, TW), f32),
             pltpu.VMEM((n_wide, cd_tiles, TW), bf16),

time: 18.5 us -> 18 us (0.973)
  Pallas kernels: 17.8 us -> 17.2 us
    pallas_call x1, Pallas kernels: 17.8 us -> 17.2 us  [per_device(): pl.pallas_call(functools.partial(kernel, n_wide, n_grp), out_shape=jax.Sh...]
where the time goes in v4:
time: 18 us; the launch traced here: 17.8 us
  Pallas kernels  17.2 us (96%)
  local copies, waits for them, and re-layouts  0.6 us (3%)
    pallas_call x1, Pallas kernels, per_device(): pl.pallas_call(functools.partial(kernel, n_wide, n_grp), out_shape=jax.Sh...  17.2 us
    unnamed x1, local copies, waits for them, and re-layouts  0.6 us

profile of v4, /device:TPU:0, one launch (start us, length us, event | category | flops | bytes accessed | tf_op | source)
XLA Modules:
  0.0 17.8 jit_solution(17646708301968434342)
XLA Ops:
  0.0 17.2 %shard_map.46 = bf16[1,2048]{1,0:T(2,128)(2,1)S(1)} custom-call(bf16[1,8192]{1,0:T(2,128)(2,1)} %amp_hbm.1, s32[32,64]{1,0:T(8,128)} %live_hbm.1, bf16[256,2048]{1,0:T(8,128)(2,1)} %int_hbm.1, s32[2,16]{1,0:T(2,128)} %int_live_hbm.1), custom_call_target="tpu_custom_call" | custom-call | flops 33554432 | bytes 1048576 | tf_op jit(solution)/shard_map/pallas_call | solution.py:171
  17.2 0.6 %copy.6 = bf16[1,2048]{1,0:T(2,128)(2,1)} copy(bf16[1,2048]{1,0:T(2,128)(2,1)S(1)} %shard_map.46) | data formatting | bytes 8192

commit v5 on v4

--- a/solution.py
+++ b/solution.py
@@ -24,7 +24,7 @@
     amp_hbm, live_hbm, int_hbm, int_live_hbm, out_ref,
     amp, live, ints, ints_t, int_live, tiles, send_buf, blocks, wide_tiles, lhs,
     partial, rows_in,
-    load_sems, recv_sems, row_sem, send_sems,
+    load_sems, send_sems, recv_sems,
 ):
     ab, cd = ints.shape
     cd_tiles, ab_tiles = cd // TW, ab // TW
@@ -61,7 +61,7 @@
     def greet(w, g):
         pl.semaphore_signal(barrier, inc=1, device_id=(w, g), device_id_type=MESH)
 
-    loop(n_wide - 1, lambda i: plane(up(wide, i + 1, n_wide), greet, 0), 8)
+    loop(n_wide - 1, lambda i: greet(up(wide, i + 1, n_wide), grp), 8)
     plane(wide, greet, 1)
 
     loads[0].wait()
@@ -77,24 +77,34 @@
 
     loop(n_wide, prepare, 4)
 
-    pl.semaphore_wait(barrier, n_wide * n_grp - 1)
-
-    def send(w, g):
+    pl.semaphore_wait(barrier, n_wide + n_grp - 2)
+
+    def send_block(w):
         pltpu.make_async_remote_copy(
             src_ref=send_buf.at[w],
-            dst_ref=blocks.at[wide, grp],
+            dst_ref=blocks.at[grp, wide],
             send_sem=send_sems.at[0],
-            recv_sem=recv_sems.at[wide],
+            recv_sem=recv_sems.at[0],
+            device_id=(w, grp),
+            device_id_type=MESH,
+        ).start()
+
+    def send_column(w, g):
+        pltpu.make_async_remote_copy(
+            src_ref=blocks.at[grp],
+            dst_ref=blocks.at[grp],
+            send_sem=send_sems.at[1],
+            recv_sem=recv_sems.at[1],
             device_id=(w, g),
             device_id_type=MESH,
         ).start()
 
     def send_row(w, g):
         pltpu.make_async_remote_copy(
-            src_ref=partial.at[w, g],
-            dst_ref=rows_in.at[wide, grp],
-            send_sem=send_sems.at[1],
-            recv_sem=row_sem,
+            src_ref=partial.at[g * n_wide + w],
+            dst_ref=rows_in.at[wide * n_grp + grp],
+            send_sem=send_sems.at[2],
+            recv_sem=recv_sems.at[2],
             device_id=(w, g),
             device_id_type=MESH,
         ).start()
@@ -102,9 +112,11 @@
     def wait_all(refs, sem):
         pltpu.make_async_copy(refs, refs, sem).wait()
 
-    loop(n_wide - 1, lambda i: plane(down(wide, i + 1, n_wide), send, 0), 8)
-    plane(wide, send, 1)
-    blocks[wide, grp] = send_buf[wide]
+    loop(n_wide - 1, lambda i: send_block(down(wide, i + 1, n_wide)), 8)
+    blocks[grp, wide] = send_buf[wide]
+    from_wide = blocks.at[0, pl.ds(0, n_wide - 1)]
+    wait_all(from_wide, recv_sems.at[0])
+    plane(wide, send_column, 1)
 
     loads[2].wait()
     loads[3].wait()
@@ -114,49 +126,47 @@
             keep = jnp.full((TW, TW), int_live[a, c].astype(jnp.float32), jnp.float32)
             ints_t[block[1], block[0]] = (ints[block] * keep.astype(jnp.bfloat16)).T
 
-    def multiply(w):
-        wide_tiles[...] = blocks[w].astype(jnp.float32).reshape(n_grp * cd_tiles, TW)
+    from_grp = blocks.at[pl.ds(0, n_grp - 1)]
+    wait_all(from_grp, recv_sems.at[1])
+
+    n = n_wide * n_grp
+    step = lhs.shape[0]
+    flat = blocks.reshape(n, cd_tiles, TW)
+
+    def multiply(i):
+        here = pl.ds(i * step, step)
+        wide_tiles[...] = flat[here].astype(jnp.float32).reshape(step * cd_tiles, TW)
         for c in range(cd_tiles):
             lhs[:, c * TW:(c + 1) * TW] = wide_tiles[
-                pl.ds(c, n_grp, stride=cd_tiles), :
-            ]
+                pl.ds(c, step, stride=cd_tiles), :
+            ].astype(jnp.bfloat16)
         total = lax.dot_general(
-            lhs[...].astype(jnp.bfloat16), ints_t[...], (((1,), (0,)), ((), ())),
+            lhs[...], ints_t[...], (((1,), (0,)), ((), ())),
             preferred_element_type=jnp.float32,
         )
-        partial[w] = total.reshape(n_grp, 1, ab)
-
-    wait_all(blocks.at[0, pl.ds(0, n_grp - 1)], recv_sems.at[wide])
-    multiply(wide)
+        partial[here] = total.reshape(step, 1, ab)
+
+    loop(n // step, multiply, 1)
+
+    loop(n_wide - 1, lambda i: plane(down(wide, i + 1, n_wide), send_row, 0), 8)
     plane(wide, send_row, 1)
-    rows_in[wide, grp] = partial[wide, grp]
-
-    def other_rows(i):
-        w = down(wide, i + 1, n_wide)
-        wait_all(blocks.at[0], recv_sems.at[w])
-        multiply(w)
-        plane(w, send_row, 0)
-
-    loop(n_wide - 1, other_rows, 8)
-
-    def wait_others(refs, sem):
-        flat = refs.reshape((n_wide * n_grp,) + refs.shape[2:])
-        wait_all(flat.at[pl.ds(0, n_wide * n_grp - 1)], sem)
-
-    wait_others(rows_in, row_sem)
+    rows_in[wide * n_grp + grp] = partial[grp * n_wide + wide]
+    from_others = rows_in.at[pl.ds(0, n - 1)]
+    wait_all(from_others, recv_sems.at[2])
     for g in range(n_grp):
         if n_wide <= 8:
-            total = rows_in[0, g]
+            total = rows_in[g]
             for w in range(1, n_wide):
-                total = total + rows_in[w, g]
+                total = total + rows_in[w * n_grp + g]
         else:
             total = lax.fori_loop(
-                1, n_wide, lambda w, s: s + rows_in[w, g], rows_in[0, g]
+                1, n_wide, lambda w, s: s + rows_in[w * n_grp + g], rows_in[g]
             )
         out_ref[:, g * ab:(g + 1) * ab] = total.astype(jnp.bfloat16)
 
-    wait_others(blocks, send_sems.at[0])
-    wait_others(rows_in, send_sems.at[1])
+    wait_all(from_wide, send_sems.at[0])
+    wait_all(from_grp, send_sems.at[1])
+    wait_all(from_others, send_sems.at[2])
 
 
 def per_device(*args):
@@ -167,6 +177,8 @@
     n_grp = lax.axis_size("grp")
     ab, cd = integrals.shape
     cd_tiles = cd // TW
+    n = n_wide * n_grp
+    step = min(n, 32)
     bf16, f32 = jnp.bfloat16, jnp.float32
     return pl.pallas_call(
         functools.partial(kernel, n_wide, n_grp),
@@ -181,15 +193,14 @@
             pltpu.SMEM(integral_live.shape, jnp.int32),
             pltpu.VMEM((cd_tiles, TW), f32),
             pltpu.VMEM((n_wide, cd_tiles, TW), bf16),
-            pltpu.VMEM((n_wide, n_grp, cd_tiles, TW), bf16),
-            pltpu.VMEM((n_grp * cd_tiles, TW), f32),
-            pltpu.VMEM((n_grp, cd), f32),
-            pltpu.VMEM((n_wide, n_grp, 1, ab), f32),
-            pltpu.VMEM((n_wide, n_grp, 1, ab), f32),
+            pltpu.VMEM((n_grp, n_wide, cd_tiles, TW), bf16),
+            pltpu.VMEM((step * cd_tiles, TW), f32),
+            pltpu.VMEM((step, cd), bf16),
+            pltpu.VMEM((n, 1, ab), f32),
+            pltpu.VMEM((n, 1, ab), f32),
             pltpu.SemaphoreType.DMA((4,)),
-            pltpu.SemaphoreType.DMA((n_wide,)),
-            pltpu.SemaphoreType.DMA,
-            pltpu.SemaphoreType.DMA((2,)),
+            pltpu.SemaphoreType.DMA((3,)),
+            pltpu.SemaphoreType.DMA((3,)),
         ],
         compiler_params=pltpu.CompilerParams(
             collective_id=0, has_side_effects=True, vmem_limit_bytes=48 * 1024 * 1024

time: 18 us -> 17.9 us (level)
  no operation moved by 1% of the time
where the time goes in v5:
time: 17.9 us; the launch traced here: 17.8 us
  Pallas kernels  17.2 us (96%)
  local copies, waits for them, and re-layouts  0.6 us (3%)
    pallas_call x1, Pallas kernels, per_device(): pl.pallas_call(functools.partial(kernel, n_wide, n_grp), out_shape=jax.Sh...  17.2 us
    unnamed x1, local copies, waits for them, and re-layouts  0.6 us

profile of v5, /device:TPU:0, one launch (start us, length us, event | category | flops | bytes accessed | tf_op | source)
XLA Modules:
  0.0 17.8 jit_solution(9183819038306735319)
XLA Ops:
  0.0 17.2 %shard_map.46 = bf16[1,2048]{1,0:T(2,128)(2,1)S(1)} custom-call(bf16[1,8192]{1,0:T(2,128)(2,1)} %amp_hbm.1, s32[32,64]{1,0:T(8,128)} %live_hbm.1, bf16[256,2048]{1,0:T(8,128)(2,1)} %int_hbm.1, s32[2,16]{1,0:T(2,128)} %int_live_hbm.1), custom_call_target="tpu_custom_call" | custom-call | flops 33554432 | bytes 1048576 | tf_op jit(solution)/shard_map/pallas_call | solution.py:183
  17.2 0.6 %copy.6 = bf16[1,2048]{1,0:T(2,128)(2,1)} copy(bf16[1,2048]{1,0:T(2,128)(2,1)S(1)} %shard_map.46) | data formatting | bytes 8192

commit v6 on v5

--- a/solution.py
+++ b/solution.py
@@ -24,7 +24,7 @@
     amp_hbm, live_hbm, int_hbm, int_live_hbm, out_ref,
     amp, live, ints, ints_t, int_live, tiles, send_buf, blocks, wide_tiles, lhs,
     partial, rows_in,
-    load_sems, send_sems, recv_sems,
+    load_sems, send_sems, recv_sems, column_sems,
 ):
     ab, cd = ints.shape
     cd_tiles, ab_tiles = cd // TW, ab // TW
@@ -39,8 +39,8 @@
         pltpu.make_async_copy(int_live_hbm, int_live, load_sems.at[2]),
         pltpu.make_async_copy(int_hbm, ints, load_sems.at[3]),
     ]
-    for load in loads:
-        load.start()
+    loads[0].start()
+    loads[1].start()
 
     barrier = pltpu.get_barrier_semaphore()
 
@@ -63,6 +63,8 @@
 
     loop(n_wide - 1, lambda i: greet(up(wide, i + 1, n_wide), grp), 8)
     plane(wide, greet, 1)
+    loads[2].start()
+    loads[3].start()
 
     loads[0].wait()
     loads[1].wait()
@@ -94,18 +96,18 @@
             src_ref=blocks.at[grp],
             dst_ref=blocks.at[grp],
             send_sem=send_sems.at[1],
-            recv_sem=recv_sems.at[1],
+            recv_sem=column_sems.at[grp],
             device_id=(w, g),
             device_id_type=MESH,
         ).start()
 
-    def send_row(w, g):
+    def send_row(w, i):
         pltpu.make_async_remote_copy(
-            src_ref=partial.at[g * n_wide + w],
+            src_ref=partial.at[i * n_wide + w],
             dst_ref=rows_in.at[wide * n_grp + grp],
             send_sem=send_sems.at[2],
             recv_sem=recv_sems.at[2],
-            device_id=(w, g),
+            device_id=(w, near[i]),
             device_id_type=MESH,
         ).start()
 
@@ -126,31 +128,36 @@
             keep = jnp.full((TW, TW), int_live[a, c].astype(jnp.float32), jnp.float32)
             ints_t[block[1], block[0]] = (ints[block] * keep.astype(jnp.bfloat16)).T
 
+    for i, g in enumerate(near):
+        if i > 0:
+            wait_all(blocks.at[0], column_sems.at[g])
+        wide_tiles[i] = blocks[g].astype(jnp.float32).reshape(n_wide * cd_tiles, TW)
+        for c in range(cd_tiles):
+            lhs[i * n_wide:(i + 1) * n_wide, c * TW:(c + 1) * TW] = wide_tiles[
+                i, pl.ds(c, n_wide, stride=cd_tiles), :
+            ]
+
+    n = n_wide * n_grp
+    step = min(n, 32)
     from_grp = blocks.at[pl.ds(0, n_grp - 1)]
-    wait_all(from_grp, recv_sems.at[1])
-
-    n = n_wide * n_grp
-    step = lhs.shape[0]
-    flat = blocks.reshape(n, cd_tiles, TW)
 
     def multiply(i):
         here = pl.ds(i * step, step)
-        wide_tiles[...] = flat[here].astype(jnp.float32).reshape(step * cd_tiles, TW)
-        for c in range(cd_tiles):
-            lhs[:, c * TW:(c + 1) * TW] = wide_tiles[
-                pl.ds(c, step, stride=cd_tiles), :
-            ].astype(jnp.bfloat16)
         total = lax.dot_general(
-            lhs[...], ints_t[...], (((1,), (0,)), ((), ())),
+            lhs[here].astype(jnp.bfloat16), ints_t[...], (((1,), (0,)), ((), ())),
             preferred_element_type=jnp.float32,
         )
         partial[here] = total.reshape(step, 1, ab)
 
     loop(n // step, multiply, 1)
 
-    loop(n_wide - 1, lambda i: plane(down(wide, i + 1, n_wide), send_row, 0), 8)
-    plane(wide, send_row, 1)
-    rows_in[wide * n_grp + grp] = partial[grp * n_wide + wide]
+    def send_rows(w, first):
+        for i in range(first, n_grp):
+            send_row(w, i)
+
+    loop(n_wide - 1, lambda j: send_rows(down(wide, j + 1, n_wide), 0), 8)
+    send_rows(wide, 1)
+    rows_in[wide * n_grp + grp] = partial[wide]
     from_others = rows_in.at[pl.ds(0, n - 1)]
     wait_all(from_others, recv_sems.at[2])
     for g in range(n_grp):
@@ -178,7 +185,6 @@
     ab, cd = integrals.shape
     cd_tiles = cd // TW
     n = n_wide * n_grp
-    step = min(n, 32)
     bf16, f32 = jnp.bfloat16, jnp.float32
     return pl.pallas_call(
         functools.partial(kernel, n_wide, n_grp),
@@ -194,13 +200,14 @@
             pltpu.VMEM((cd_tiles, TW), f32),
             pltpu.VMEM((n_wide, cd_tiles, TW), bf16),
             pltpu.VMEM((n_grp, n_wide, cd_tiles, TW), bf16),
-            pltpu.VMEM((step * cd_tiles, TW), f32),
-            pltpu.VMEM((step, cd), bf16),
+            pltpu.VMEM((n_grp, n_wide * cd_tiles, TW), f32),
+            pltpu.VMEM((n, cd), f32),
             pltpu.VMEM((n, 1, ab), f32),
             pltpu.VMEM((n, 1, ab), f32),
             pltpu.SemaphoreType.DMA((4,)),
             pltpu.SemaphoreType.DMA((3,)),
             pltpu.SemaphoreType.DMA((3,)),
+            pltpu.SemaphoreType.DMA((n_grp,)),
         ],
         compiler_params=pltpu.CompilerParams(
             collective_id=0, has_side_effects=True, vmem_limit_bytes=48 * 1024 * 1024

time: 17.9 us -> 18.1 us (1.011)
  no operation moved by 1% of the time
where the time goes in v6:
time: 18.1 us; the launch traced here: 18 us
  Pallas kernels  17.3 us (96%)
  local copies, waits for them, and re-layouts  0.6 us (3%)
    pallas_call x1, Pallas kernels, per_device(): pl.pallas_call(functools.partial(kernel, n_wide, n_grp), out_shape=jax.Sh...  17.3 us
    unnamed x1, local copies, waits for them, and re-layouts  0.6 us

profile of v6, /device:TPU:0, one launch (start us, length us, event | category | flops | bytes accessed | tf_op | source)
XLA Modules:
  0.0 18.0 jit_solution(16006083773554743907)
XLA Ops:
  0.0 17.3 %shard_map.46 = bf16[1,2048]{1,0:T(2,128)(2,1)S(1)} custom-call(bf16[1,8192]{1,0:T(2,128)(2,1)} %amp_hbm.1, s32[32,64]{1,0:T(8,128)} %live_hbm.1, bf16[256,2048]{1,0:T(8,128)(2,1)} %int_hbm.1, s32[2,16]{1,0:T(2,128)} %int_live_hbm.1), custom_call_target="tpu_custom_call" | custom-call | flops 33554432 | bytes 1048576 | tf_op jit(solution)/shard_map/pallas_call | solution.py:189
  17.3 0.6 %copy.6 = bf16[1,2048]{1,0:T(2,128)(2,1)} copy(bf16[1,2048]{1,0:T(2,128)(2,1)S(1)} %shard_map.46) | data formatting | bytes 8192

commit v7 on v4

--- a/solution.py
+++ b/solution.py
@@ -24,7 +24,7 @@
     amp_hbm, live_hbm, int_hbm, int_live_hbm, out_ref,
     amp, live, ints, ints_t, int_live, tiles, send_buf, blocks, wide_tiles, lhs,
     partial, rows_in,
-    load_sems, recv_sems, row_sem, send_sems,
+    load_sems, recv_sems, row_sem, forward_sems, send_sems,
 ):
     ab, cd = ints.shape
     cd_tiles, ab_tiles = cd // TW, ab // TW
@@ -52,17 +52,22 @@
         there = index - i
         return jnp.where(there < 0, there + count, there)
 
+    half = n_grp // 2
+    core, chip = lax.rem(grp, 2), grp // 2
     near = [up(grp, i, n_grp) for i in range(n_grp)]
-
-    def plane(w, body, first):
-        for g in near[first:]:
-            body(w, g)
+    same_core = [up(chip, i, half) * 2 + core for i in range(half)]
+    partner = chip * 2 + 1 - core
 
     def greet(w, g):
         pl.semaphore_signal(barrier, inc=1, device_id=(w, g), device_id_type=MESH)
 
+    def plane(w, body, first):
+        for g in same_core[first:]:
+            body(w, g)
+
     loop(n_wide - 1, lambda i: plane(up(wide, i + 1, n_wide), greet, 0), 8)
     plane(wide, greet, 1)
+    greet(wide, partner)
 
     loads[0].wait()
     loads[1].wait()
@@ -77,21 +82,31 @@
 
     loop(n_wide, prepare, 4)
 
-    pl.semaphore_wait(barrier, n_wide * n_grp - 1)
+    pl.semaphore_wait(barrier, n_wide * half)
 
     def send(w, g):
         pltpu.make_async_remote_copy(
             src_ref=send_buf.at[w],
-            dst_ref=blocks.at[wide, grp],
+            dst_ref=blocks.at[wide, core, chip],
             send_sem=send_sems.at[0],
             recv_sem=recv_sems.at[wide],
             device_id=(w, g),
             device_id_type=MESH,
         ).start()
 
+    def forward(w):
+        pltpu.make_async_remote_copy(
+            src_ref=blocks.at[w, core],
+            dst_ref=blocks.at[w, core],
+            send_sem=send_sems.at[2],
+            recv_sem=forward_sems.at[w],
+            device_id=(wide, partner),
+            device_id_type=MESH,
+        ).start()
+
     def send_row(w, g):
         pltpu.make_async_remote_copy(
-            src_ref=partial.at[w, g],
+            src_ref=partial.at[w, lax.rem(g, 2) * half + g // 2],
             dst_ref=rows_in.at[wide, grp],
             send_sem=send_sems.at[1],
             recv_sem=row_sem,
@@ -104,7 +119,7 @@
 
     loop(n_wide - 1, lambda i: plane(down(wide, i + 1, n_wide), send, 0), 8)
     plane(wide, send, 1)
-    blocks[wide, grp] = send_buf[wide]
+    blocks[wide, core, chip] = send_buf[wide]
 
     loads[2].wait()
     loads[3].wait()
@@ -126,24 +141,33 @@
         )
         partial[w] = total.reshape(n_grp, 1, ab)
 
-    wait_all(blocks.at[0, pl.ds(0, n_grp - 1)], recv_sems.at[wide])
-    multiply(wide)
-    plane(wide, send_row, 1)
-    rows_in[wide, grp] = partial[wide, grp]
+    def finish(w, first):
+        wait_all(blocks.at[0, 0], forward_sems.at[w])
+        multiply(w)
+        for g in near[first:]:
+            send_row(w, g)
+
+    def arrive(i):
+        w = down(wide, i, n_wide)
+        wait_all(blocks.at[0, 0], recv_sems.at[w])
+        forward(w)
+
+    wait_all(blocks.at[0, 0, pl.ds(0, half - 1)], recv_sems.at[wide])
+    forward(wide)
+    arrive(1)
+    finish(wide, 1)
+    rows_in[wide, grp] = partial[wide, core * half + chip]
 
     def other_rows(i):
-        w = down(wide, i + 1, n_wide)
-        wait_all(blocks.at[0], recv_sems.at[w])
-        multiply(w)
-        plane(w, send_row, 0)
-
-    loop(n_wide - 1, other_rows, 8)
-
-    def wait_others(refs, sem):
-        flat = refs.reshape((n_wide * n_grp,) + refs.shape[2:])
-        wait_all(flat.at[pl.ds(0, n_wide * n_grp - 1)], sem)
-
-    wait_others(rows_in, row_sem)
+        arrive(i + 2)
+        finish(down(wide, i + 1, n_wide), 0)
+
+    loop(n_wide - 2, other_rows, 8)
+    finish(down(wide, n_wide - 1, n_wide), 0)
+
+    n = n_wide * n_grp
+    others = rows_in.reshape(n, 1, ab).at[pl.ds(0, n - 1)]
+    wait_all(others, row_sem)
     for g in range(n_grp):
         if n_wide <= 8:
             total = rows_in[0, g]
@@ -155,8 +179,10 @@
             )
         out_ref[:, g * ab:(g + 1) * ab] = total.astype(jnp.bfloat16)
 
-    wait_others(blocks, send_sems.at[0])
-    wait_others(rows_in, send_sems.at[1])
+    sent = blocks.reshape(n, cd_tiles, TW)
+    wait_all(sent.at[pl.ds(0, n // 2 - 1)], send_sems.at[0])
+    wait_all(others, send_sems.at[1])
+    wait_all(sent.at[pl.ds(0, n // 2)], send_sems.at[2])
 
 
 def per_device(*args):
@@ -181,7 +207,7 @@
             pltpu.SMEM(integral_live.shape, jnp.int32),
             pltpu.VMEM((cd_tiles, TW), f32),
             pltpu.VMEM((n_wide, cd_tiles, TW), bf16),
-            pltpu.VMEM((n_wide, n_grp, cd_tiles, TW), bf16),
+            pltpu.VMEM((n_wide, 2, n_grp // 2, cd_tiles, TW), bf16),
             pltpu.VMEM((n_grp * cd_tiles, TW), f32),
             pltpu.VMEM((n_grp, cd), f32),
             pltpu.VMEM((n_wide, n_grp, 1, ab), f32),
@@ -189,7 +215,8 @@
             pltpu.SemaphoreType.DMA((4,)),
             pltpu.SemaphoreType.DMA((n_wide,)),
             pltpu.SemaphoreType.DMA,
-            pltpu.SemaphoreType.DMA((2,)),
+            pltpu.SemaphoreType.DMA((n_wide,)),
+            pltpu.SemaphoreType.DMA((3,)),
         ],
         compiler_params=pltpu.CompilerParams(
             collective_id=0, has_side_effects=True, vmem_limit_bytes=48 * 1024 * 1024

time: 18 us -> 17.6 us (0.978)
  Pallas kernels: 17.2 us -> 16.9 us
    pallas_call x1, Pallas kernels: 17.2 us -> 16.9 us  [per_device(): pl.pallas_call(functools.partial(kernel, n_wide, n_grp), out_shape=jax.Sh...]
where the time goes in v7:
time: 17.6 us; the launch traced here: 17.5 us
  Pallas kernels  16.9 us (96%)
  local copies, waits for them, and re-layouts  0.6 us (3%)
    pallas_call x1, Pallas kernels, per_device(): pl.pallas_call(functools.partial(kernel, n_wide, n_grp), out_shape=jax.Sh...  16.9 us
    unnamed x1, local copies, waits for them, and re-layouts  0.6 us

profile of v7, /device:TPU:0, one launch (start us, length us, event | category | flops | bytes accessed | tf_op | source)
XLA Modules:
  0.0 17.5 jit_solution(832433769378434658)
XLA Ops:
  0.0 16.9 %shard_map.46 = bf16[1,2048]{1,0:T(2,128)(2,1)S(1)} custom-call(bf16[1,8192]{1,0:T(2,128)(2,1)} %amp_hbm.1, s32[32,64]{1,0:T(8,128)} %live_hbm.1, bf16[256,2048]{1,0:T(8,128)(2,1)} %int_hbm.1, s32[2,16]{1,0:T(2,128)} %int_live_hbm.1), custom_call_target="tpu_custom_call" | custom-call | flops 33554432 | bytes 1048576 | tf_op jit(solution)/shard_map/pallas_call | solution.py:197
  16.9 0.6 %copy.6 = bf16[1,2048]{1,0:T(2,128)(2,1)} copy(bf16[1,2048]{1,0:T(2,128)(2,1)S(1)} %shard_map.46) | data formatting | bytes 8192
